TPU v7x, 32 devices: a whole 2x2x4 slice. The times are simulated.
32 devices in a mesh: gx: 4 (over y, core), gy: 8 (over z, x).
Axes of the slice: x: 2, y: 2, z: 4, core: 2. Of those that a mesh axis runs over, the one named last changes fastest.
Arguments:
- skip_input: bfloat16 [32, 16, 2048], P(None, 'gx', 'gy'), may hold values from -6 to 6
- w_encoder: bfloat16 [64, 864], replicated, may hold values from -0.625 to 0.625
- w_bottom: bfloat16 [128, 1728], P('gx'), may hold values from -0.3125 to 0.3125
- w_middle: bfloat16 [64, 5184], replicated, may hold values from -0.15625 to 0.15625
- w_upper: bfloat16 [32, 2592], replicated, may hold values from -0.21875 to 0.21875
- cotangent: bfloat16 [32, 16, 2048], P(None, 'gx', 'gy'), may hold values from -6 to 6
Outputs:
- features: bfloat16 [32, 16, 2048], P(None, 'gx', 'gy')
- grad_skip: bfloat16 [32, 16, 2048], P(None, 'gx', 'gy')
- grad_encoder: float32 [64, 864], replicated
- grad_bottom: float32 [128, 1728], P('gx')
- grad_middle: float32 [64, 5184], replicated
- grad_upper: float32 [32, 2592], replicated
All inputs are finite; a program needn't handle non-finite values.
Results may differ from a plain program's by a relative error of at most 0.017.
Values may be sent and summed in bfloat16 or wider, within the bound.
A program may use at most 64 MiB of HBM per device.

v0:
```python
import math

import jax
import jax.numpy as jnp
from jax import lax
from jax.sharding import PartitionSpec as P

Z = 16


def extended_2(cells, sides, width):
    for axis, dim in sides:
        count = lax.axis_size(axis)
        ends = count - 1
        head = lax.slice_in_dim(cells, 0, width, axis=dim)
        tail = lax.slice_in_dim(cells, cells.shape[dim] - width, cells.shape[dim], axis=dim)
        cells = jnp.concatenate(
            [
                lax.ppermute(tail, axis, [(i, (i + 1) % count) for i in range(ends)]),
                cells,
                lax.ppermute(head, axis, [((i + 1) % count, i) for i in range(ends)]),
            ],
            axis=dim,
        )
    return cells


def z_shift(extended, z_step, z_depth):
    length = extended.shape[2]
    padded = jnp.pad(extended, ((0, 0), (0, 0), (1, 1)))
    shifted = padded[:, :, 1 + z_step : 1 + z_step + length]
    z_index = lax.broadcasted_iota(jnp.int32, (1, 1, length), 2) % z_depth + z_step
    inside = (z_index >= 0) & (z_index < z_depth)
    return jnp.where(inside, shifted, jnp.zeros_like(shifted))


def tap_piece(shifted_set, a, b, c, row_count, col_count, z_depth, flipped):
    x_off, y_off, z_off = (2 - a, 2 - b, 2 - c) if flipped else (a, b, c)
    source = shifted_set[z_off]
    tap_slice = source[
        :, x_off : x_off + row_count, y_off * z_depth : (y_off + col_count) * z_depth
    ]
    return tap_slice.reshape(source.shape[0], row_count * col_count * z_depth)


def conv_forward(extended, weight, row_count, col_count, z_depth):
    in_chan = extended.shape[0]
    shifted_set = [z_shift(extended, z_step, z_depth) for z_step in (-1, 0, 1)]
    total_sum = jnp.zeros((weight.shape[0], row_count * col_count * z_depth), jnp.float32)
    for a in range(3):
        for b in range(3):
            for c in range(3):
                tap_number = 9 * a + 3 * b + c
                total_sum = total_sum + jnp.dot(
                    weight[:, tap_number * in_chan : (tap_number + 1) * in_chan],
                    tap_piece(shifted_set, a, b, c, row_count, col_count, z_depth, False),
                    preferred_element_type=jnp.float32,
                )
    return total_sum


def conv_backward(extended, weight, row_count, col_count, z_depth):
    in_chan = weight.shape[1] // 27
    shifted_set = [z_shift(extended, z_step, z_depth) for z_step in (-1, 0, 1)]
    total_sum = jnp.zeros((in_chan, row_count * col_count * z_depth), jnp.float32)
    for a in range(3):
        for b in range(3):
            for c in range(3):
                tap_number = 9 * a + 3 * b + c
                total_sum = total_sum + lax.dot_general(
                    weight[:, tap_number * in_chan : (tap_number + 1) * in_chan],
                    tap_piece(shifted_set, a, b, c, row_count, col_count, z_depth, True),
                    (((0,), (0,)), ((), ())),
                    preferred_element_type=jnp.float32,
                )
    return total_sum


def weight_grad(extended, error_flat, row_count, col_count, z_depth):
    shifted_set = [z_shift(extended, z_step, z_depth) for z_step in (-1, 0, 1)]
    blocks = []
    for a in range(3):
        for b in range(3):
            for c in range(3):
                blocks.append(
                    lax.dot_general(
                        error_flat,
                        tap_piece(shifted_set, a, b, c, row_count, col_count, z_depth, False),
                        (((1,), (1,)), ((), ())),
                        preferred_element_type=jnp.float32,
                    )
                )
    return jnp.concatenate(blocks, axis=1)


def pool_mean(values, z_depth):
    channels, row_count, length = values.shape
    col_count = length // z_depth
    shaped = values.astype(jnp.float32).reshape(
        channels, row_count // 2, 2, col_count // 2, 2, z_depth // 2, 2
    )
    return shaped.mean(axis=(2, 4, 6)).reshape(
        channels, row_count // 2, col_count // 2 * (z_depth // 2)
    )


def block_sum(values, z_depth):
    channels, row_count, length = values.shape
    col_count = length // z_depth
    shaped = values.reshape(channels, row_count // 2, 2, col_count // 2, 2, z_depth // 2, 2)
    return shaped.sum(axis=(2, 4, 6)).reshape(
        channels, row_count // 2, col_count // 2 * (z_depth // 2)
    )


def upsample(values, z_depth):
    channels, row_count, length = values.shape
    col_count = length // z_depth
    shaped = values.reshape(channels, row_count, 1, col_count, 1, z_depth, 1)
    shaped = jnp.broadcast_to(shaped, (channels, row_count, 2, col_count, 2, z_depth, 2))
    return shaped.reshape(channels, 2 * row_count, 4 * col_count * z_depth)


def silu_slope(values):
    s_value = jax.nn.sigmoid(values)
    return s_value * (1.0 + values * (1.0 - s_value))


def spatial_halo(values, z_depth):
    widened = extended_2(values, (("gy", 2),), z_depth)
    return extended_2(widened, (("gx", 1),), 1)


def per_device(skip_input, w_encoder, w_bottom, w_middle, w_upper, cotangent):
    top_chan = skip_input.shape[0]
    rows_fine = skip_input.shape[1]
    cols_fine = skip_input.shape[2] // Z
    rows_mid, cols_mid, depth_mid = (rows_fine // 2, cols_fine // 2, Z // 2)
    rows_low, cols_low, depth_low = (rows_fine // 4, cols_fine // 4, Z // 4)
    cells_fine = rows_fine * cols_fine * Z * lax.axis_size("gx") * lax.axis_size("gy")
    scale_fine = 1.0 / math.sqrt(cells_fine)
    scale_mid = 1.0 / math.sqrt(cells_fine // 8)
    scale_low = 1.0 / math.sqrt(cells_fine // 64)
    pool_top = pool_mean(skip_input, Z).astype(jnp.bfloat16)
    ext_pool = spatial_halo(pool_top, depth_mid)
    pre_one = conv_forward(ext_pool, w_encoder, rows_mid, cols_mid, depth_mid)
    act_one = jax.nn.silu(pre_one).astype(jnp.bfloat16).reshape(-1, rows_mid, cols_mid * depth_mid)
    pool_mid = pool_mean(act_one, depth_mid).astype(jnp.bfloat16)
    col_ext = extended_2(pool_mid, (("gy", 2),), depth_low)
    whole_rows = lax.all_gather(col_ext, "gx", axis=1, tiled=True)
    ext_low = jnp.pad(whole_rows, ((0, 0), (1, 1), (0, 0)))
    rows_all = whole_rows.shape[1]
    pre_two = conv_forward(ext_low, w_bottom, rows_all, cols_low, depth_low)
    act_block = (
        jax.nn.silu(pre_two).astype(jnp.bfloat16).reshape(-1, rows_all, cols_low * depth_low)
    )
    act_two = lax.all_to_all(act_block, "gx", split_axis=1, concat_axis=0, tiled=True)
    cat_mid = jnp.concatenate([upsample(act_two, depth_low), act_one], axis=0)
    ext_mid = spatial_halo(cat_mid, depth_mid)
    pre_three = conv_forward(ext_mid, w_middle, rows_mid, cols_mid, depth_mid)
    act_three = (
        jax.nn.silu(pre_three).astype(jnp.bfloat16).reshape(-1, rows_mid, cols_mid * depth_mid)
    )
    cat_top = jnp.concatenate([upsample(act_three, depth_mid), skip_input], axis=0)
    ext_top = spatial_halo(cat_top, Z)
    pre_four = conv_forward(ext_top, w_upper, rows_fine, cols_fine, Z)
    features = (
        jax.nn.silu(pre_four).astype(jnp.bfloat16).reshape(top_chan, rows_fine, cols_fine * Z)
    )
    err_four = (cotangent.reshape(top_chan, -1).astype(jnp.float32) * silu_slope(pre_four)).astype(
        jnp.bfloat16
    )
    local_upper = weight_grad(ext_top, err_four, rows_fine, cols_fine, Z) * scale_fine
    grad_upper = lax.psum(local_upper, ("gx", "gy"))
    dcat_top = conv_backward(
        spatial_halo(err_four.reshape(top_chan, rows_fine, cols_fine * Z), Z),
        w_upper,
        rows_fine,
        cols_fine,
        Z,
    ).reshape(-1, rows_fine, cols_fine * Z)
    mid_chan = act_three.shape[0]
    err_three = (
        block_sum(dcat_top[:mid_chan], Z).reshape(mid_chan, -1) * silu_slope(pre_three)
    ).astype(jnp.bfloat16)
    local_middle = weight_grad(ext_mid, err_three, rows_mid, cols_mid, depth_mid) * scale_mid
    grad_middle = lax.psum(local_middle, ("gx", "gy"))
    dcat_mid = conv_backward(
        spatial_halo(err_three.reshape(mid_chan, rows_mid, cols_mid * depth_mid), depth_mid),
        w_middle,
        rows_mid,
        cols_mid,
        depth_mid,
    ).reshape(-1, rows_mid, cols_mid * depth_mid)
    low_chan = act_two.shape[0]
    dact_two = block_sum(dcat_mid[:low_chan], depth_mid)
    dact_block = lax.all_to_all(dact_two, "gx", split_axis=0, concat_axis=1, tiled=True)
    block_chan = dact_block.shape[0]
    err_two = (dact_block.reshape(block_chan, -1) * silu_slope(pre_two)).astype(jnp.bfloat16)
    part_bottom = weight_grad(ext_low, err_two, rows_all, cols_low, depth_low)
    err_grid = err_two.reshape(block_chan, rows_all, cols_low * depth_low)
    err_cols = extended_2(err_grid, (("gy", 2),), depth_low)
    err_ext = jnp.pad(err_cols, ((0, 0), (1, 1), (0, 0)))
    partial_sum = conv_backward(err_ext, w_bottom, rows_all, cols_low, depth_low).reshape(
        -1, rows_all, cols_low * depth_low
    )
    dpool_mid = lax.psum_scatter(
        partial_sum.astype(jnp.bfloat16), "gx", scatter_dimension=1, tiled=True
    ).astype(jnp.float32)
    grad_bottom = lax.psum((part_bottom * scale_low).astype(jnp.bfloat16), "gy").astype(jnp.float32)
    dact_one = dcat_mid[low_chan:] + upsample(dpool_mid, depth_low) / 8.0
    err_one = (dact_one.reshape(mid_chan, -1) * silu_slope(pre_one)).astype(jnp.bfloat16)
    local_encoder = weight_grad(ext_pool, err_one, rows_mid, cols_mid, depth_mid) * scale_mid
    grad_encoder = lax.psum(local_encoder, ("gx", "gy"))
    dpool_top = conv_backward(
        spatial_halo(err_one.reshape(mid_chan, rows_mid, cols_mid * depth_mid), depth_mid),
        w_encoder,
        rows_mid,
        cols_mid,
        depth_mid,
    ).reshape(-1, rows_mid, cols_mid * depth_mid)
    grad_skip = (dcat_top[mid_chan:] + upsample(dpool_top, depth_mid) / 8.0).astype(jnp.bfloat16)
    return (features, grad_skip, grad_encoder, grad_bottom, grad_middle, grad_upper)


def solution(mesh):
    in_specs = (P(None, "gx", "gy"), P(), P("gx", None), P(), P(), P(None, "gx", "gy"))
    out_specs = (P(None, "gx", "gy"), P(None, "gx", "gy"), P(), P("gx", None), P(), P())
    return jax.shard_map(
        per_device, mesh=mesh, in_specs=in_specs, out_specs=out_specs, check_vma=False
    )
```

profile of v0, /device:TPU:3, one launch (start us, length us, event | category | flops | bytes accessed | tf_op | source)
XLA Modules:
  0.0 448.2 jit_solution(14841922563857560926)
XLA Ops:
  9.4 3.2 collective-permute-start
  12.6 2.1 collective-permute-start.1
  16.0 1.9 collective-permute-done.1
  18.1 5.1 %collective-permute-start.2 = (bf16[32,1,80]{2,0,1:T(8,128)(2,1)S(1)}, bf16[32,1,80]{2,0,1:T(8,128)(2,1)S(1)}, u32[]{:S(2)}, u32[]{:S(2)}) collective-permute-start(bf16[32,1,80]{2,0,1:T(8,128)(2,1)S(1)} %get-tuple-element.307), channel_id=1, source_target_pairs={{0,8},{8,16},{16,24},{1,9},{9,17},{17,25},{2,10},{10,18},{18,26},{... | collective-permute-start | bytes 15368 | tf_op jit(solution)/shard_map/ppermute | solution.py:19
  23.2 1.9 collective-permute-start.3
  25.7 2.5 collective-permute-done.3
  38.5 2.2 collective-permute-start.4
  40.7 3.1 collective-permute-start.5
  43.8 2.1 collective-permute-done.5
  46.0 4.9 %all_gather.3 = bf16[64,4,24]{0,2,1:T(8,128)(2,1)S(1)} all-gather(bf16[64,1,24]{0,2,1:T(8,128)(2,1)S(1)} %pad_maximum_fusion.19), channel_id=1, replica_groups=mesh['gx'=4,'gy'=8] {'gx'}, dimensions={1}, use_global_device_ids=true | all-gather | bytes 15360 | tf_op jit(solution)/shard_map/all_gather | solution.py:150
  57.3 3.4 all-to-all-start
  60.9 3.0 all-to-all-done
  64.1 3.2 collective-permute-start.6
  67.3 2.1 collective-permute-start.7
  69.4 3.1 collective-permute-done.7
  72.7 3.7 collective-permute-start.8
  76.4 1.9 collective-permute-start.9
  78.4 3.3 collective-permute-done.9
  90.6 2.2 collective-permute-start.10
  92.8 3.1 collective-permute-start.11
  95.9 2.3 collective-permute-done.11
  98.3 3.3 collective-permute-start.12
  101.7 2.1 collective-permute-start.13
  103.8 3.5 collective-permute-done.13
  120.9 3.2 collective-permute-start.14
  124.1 2.1 collective-permute-start.15
  126.6 3.0 collective-permute-done.15
  129.9 3.3 collective-permute-start.16
  133.2 1.9 collective-permute-start.17
  136.6 2.1 collective-permute-done.17
  167.8 2.2 collective-permute-start.18
  170.0 3.3 collective-permute-start.19
  173.5 2.1 collective-permute-done.19
  176.4 3.3 collective-permute-start.20
  179.7 1.9 collective-permute-start.21
  199.8 3.2 all-to-all-start.1
  209.3 1.9 collective-permute-start.22
  211.2 3.4 collective-permute-start.23
  222.5 17.5 %reduce-scatter.2.cloned.1.call-done = bf16[64,1,16]{0,2,1:T(8,128)(2,1)} async-done(((bf16[64,4,16]{0,2,1:T(8,128)(2,1)}), bf16[64,1,16]{0,2,1:T(8,128)(2,1)}) %reduce-scatter.2.cloned.1.call-update) | async-done | bytes 2064 | tf_op jit(solution)/shard_map/reduce_scatter | solution.py:207
  241.2 3.1 collective-permute-start.24
  244.3 2.2 collective-permute-start.25
  250.3 4.2 collective-permute-start.26
  254.5 2.2 collective-permute-start.27
  257.5 2.2 collective-permute-done.27
  272.6 20.6 %all-reduce.14.cloned.1.call-done = bf16[32,1728]{1,0:T(8,128)(2,1)} async-done(((bf16[32,1728]{1,0:T(8,128)(2,1)}), bf16[32,1728]{1,0:T(8,128)(2,1)}) %all-reduce.14.cloned.1.call-update) | async-done | bytes 110608 | tf_op jit(solution)/shard_map/psum | solution.py:210
  294.8 140.9 %all-reduce.16.cloned.1.call-done = (f32[64,864]{0,1:T(8,128)}, f32[64,5184]{1,0:T(8,128)}, f32[32,2592]{1,0:T(8,128)}) async-done(((f32[64,864]{0,1:T(8,128)}, f32[64,5184]{1,0:T(8,128)}, f32[32,2592]{1,0:T(8,128)}), (f32[64,864]{0,1:T(8,128)}, f32[64,5184]{1,0:T(8,128)}, f32[32,2592]{1,0:T(8,128)})) %all-reduce.16.cloned.1.call-update) | async-done | bytes 1880080 | tf_op jit(solution)/shard_map/psum | solution.py:214
  435.6 1.9 copy.104
  437.5 2.5 copy.167
  (956 shorter events, 125.9 us)
Async XLA Ops:
  9.4 6.5 %collective-permute-start = (bf16[32,2,8]{0,2,1:T(8,128)(2,1)S(1)}, bf16[32,2,8]{0,2,1:T(8,128)(2,1)S(1)}, u32[]{:S(2)}, u32[]{:S(2)}) collective-permute-start(bf16[32,2,8]{0,2,1:T(8,128)(2,1)S(1)} %get-tuple-element.301), channel_id=1, source_target_pairs={{0,1},{1,2},{2,3},{3,4},{4,5},{5,6},{6,7},{8,9},{9,10},{10,11},{11... | collective-permute-start | bytes 3080 | tf_op jit(solution)/shard_map/ppermute | solution.py:19
  12.6 5.3 %collective-permute-start.1 = (bf16[32,2,8]{0,2,1:T(8,128)(2,1)S(1)}, bf16[32,2,8]{0,2,1:T(8,128)(2,1)S(1)}, u32[]{:S(2)}, u32[]{:S(2)}) collective-permute-start(bf16[32,2,8]{0,2,1:T(8,128)(2,1)S(1)} %get-tuple-element.302), channel_id=1, source_target_pairs={{1,0},{2,1},{3,2},{4,3},{5,4},{6,5},{7,6},{9,8},{10,9},{11,10},{12... | collective-permute-start | bytes 3080 | tf_op jit(solution)/shard_map/ppermute | solution.py:21
  15.3 35.7 %copy-start.160 = (pred[24]{0:T(512)(128)(4,1)}, pred[24]{0:T(512)(128)(4,1)S(1)}, u32[]{:S(2)}) copy-start(pred[24]{0:T(512)(128)(4,1)S(1)} %get-tuple-element.326) | copy-start | bytes 76
  15.3 35.7 %copy-start.162 = (pred[24]{0:T(512)(128)(4,1)}, pred[24]{0:T(512)(128)(4,1)S(1)}, u32[]{:S(2)}) copy-start(pred[24]{0:T(512)(128)(4,1)S(1)} %get-tuple-element.327) | copy-start | bytes 76
  18.1 7.7 %collective-permute-start.2 = (bf16[32,1,80]{2,0,1:T(8,128)(2,1)S(1)}, bf16[32,1,80]{2,0,1:T(8,128)(2,1)S(1)}, u32[]{:S(2)}, u32[]{:S(2)}) collective-permute-start(bf16[32,1,80]{2,0,1:T(8,128)(2,1)S(1)} %get-tuple-element.307), channel_id=1, source_target_pairs={{0,8},{8,16},{16,24},{1,9},{9,17},{17,25},{2,10},{10,18},{18,26},{... | collective-permute-start | bytes 15368 | tf_op jit(solution)/shard_map/ppermute | solution.py:19
  23.2 5.0 %collective-permute-start.3 = (bf16[32,1,80]{2,0,1:T(8,128)(2,1)S(1)}, bf16[32,1,80]{2,0,1:T(8,128)(2,1)S(1)}, u32[]{:S(2)}, u32[]{:S(2)}) collective-permute-start(bf16[32,1,80]{2,0,1:T(8,128)(2,1)S(1)} %get-tuple-element.308), channel_id=1, source_target_pairs={{8,0},{16,8},{24,16},{9,1},{17,9},{25,17},{10,2},{18,10},{26,18},{... | collective-permute-start | bytes 15368 | tf_op jit(solution)/shard_map/ppermute | solution.py:21
  38.5 5.3 %collective-permute-start.4 = (bf16[64,1,4]{0,2,1:T(4,128)(2,1)S(1)}, bf16[64,1,4]{0,2,1:T(4,128)(2,1)S(1)}, u32[]{:S(2)}, u32[]{:S(2)}) collective-permute-start(bf16[64,1,4]{0,2,1:T(4,128)(2,1)S(1)} %get-tuple-element.309), channel_id=1, source_target_pairs={{0,1},{1,2},{2,3},{3,4},{4,5},{5,6},{6,7},{8,9},{9,10},{10,11},{11... | collective-permute-start | bytes 1544 | tf_op jit(solution)/shard_map/ppermute | solution.py:19
  40.7 5.2 %collective-permute-start.5 = (bf16[64,1,4]{0,2,1:T(4,128)(2,1)S(1)}, bf16[64,1,4]{0,2,1:T(4,128)(2,1)S(1)}, u32[]{:S(2)}, u32[]{:S(2)}) collective-permute-start(bf16[64,1,4]{0,2,1:T(4,128)(2,1)S(1)} %get-tuple-element.310), channel_id=1, source_target_pairs={{1,0},{2,1},{3,2},{4,3},{5,4},{6,5},{7,6},{9,8},{10,9},{11,10},{12... | collective-permute-start | bytes 1544 | tf_op jit(solution)/shard_map/ppermute | solution.py:21
  51.3 31.1 %copy-start.70 = (bf16[64,4,16]{0,2,1:T(8,128)(2,1)}, bf16[64,4,16]{0,2,1:T(8,128)(2,1)S(1)}, u32[]{:S(2)}) copy-start(bf16[64,4,16]{0,2,1:T(8,128)(2,1)S(1)} %get-tuple-element.248) | copy-start | bytes 24580
  51.3 31.1 %copy-start.76 = (bf16[64,4,16]{0,2,1:T(8,128)(2,1)}, bf16[64,4,16]{0,2,1:T(8,128)(2,1)S(1)}, u32[]{:S(2)}) copy-start(bf16[64,4,16]{0,2,1:T(8,128)(2,1)S(1)} %get-tuple-element.247) | copy-start | bytes 24580
  51.4 31.0 %copy-start.78 = (bf16[64,4,16]{0,2,1:T(8,128)(2,1)}, bf16[64,4,16]{0,2,1:T(8,128)(2,1)S(1)}, u32[]{:S(2)}) copy-start(bf16[64,4,16]{0,2,1:T(8,128)(2,1)S(1)} %get-tuple-element.258) | copy-start | bytes 24580
  57.3 6.5 %all-to-all-start = ((bf16[4,2,256]{2,1,0:T(2,128)(2,1)}), bf16[4,2,256]{2,1,0:T(2,128)(2,1)S(1)}, u32[]{:S(2)}, u32[]{:S(2)}) async-start(bf16[4,2,256]{2,1,0:T(2,128)(2,1)} %reshape.1246), calls=%async_computation | async-start | bytes 8192 | tf_op jit(solution)/shard_map/all_to_all | solution.py:157
  64.1 5.3 %collective-permute-start.6 = (bf16[192,2,8]{0,2,1:T(8,128)(2,1)S(1)}, bf16[192,2,8]{0,2,1:T(8,128)(2,1)S(1)}, u32[]{:S(2)}, u32[]{:S(2)}) collective-permute-start(bf16[192,2,8]{0,2,1:T(8,128)(2,1)S(1)} %get-tuple-element.204), channel_id=1, source_target_pairs={{0,1},{1,2},{2,3},{3,4},{4,5},{5,6},{6,7},{8,9},{9,10},{10,11},{11... | collective-permute-start | bytes 18440 | tf_op jit(solution)/shard_map/ppermute | solution.py:19
  67.3 5.3 %collective-permute-start.7 = (bf16[192,2,8]{0,2,1:T(8,128)(2,1)S(1)}, bf16[192,2,8]{0,2,1:T(8,128)(2,1)S(1)}, u32[]{:S(2)}, u32[]{:S(2)}) collective-permute-start(bf16[192,2,8]{0,2,1:T(8,128)(2,1)S(1)} %get-tuple-element.205), channel_id=1, source_target_pairs={{1,0},{2,1},{3,2},{4,3},{5,4},{6,5},{7,6},{9,8},{10,9},{11,10},{12... | collective-permute-start | bytes 18440 | tf_op jit(solution)/shard_map/ppermute | solution.py:21
  72.7 5.6 %collective-permute-start.8 = (bf16[192,1,80]{0,2,1:T(8,128)(2,1)S(1)}, bf16[192,1,80]{0,2,1:T(8,128)(2,1)S(1)}, u32[]{:S(2)}, u32[]{:S(2)}) collective-permute-start(bf16[192,1,80]{0,2,1:T(8,128)(2,1)S(1)} %get-tuple-element.142), channel_id=1, source_target_pairs={{0,8},{8,16},{16,24},{1,9},{9,17},{17,25},{2,10},{10,18},{18,26},{... | collective-permute-start | bytes 92168 | tf_op jit(solution)/shard_map/ppermute | solution.py:19
  76.4 5.3 %collective-permute-start.9 = (bf16[192,1,80]{0,2,1:T(8,128)(2,1)S(1)}, bf16[192,1,80]{0,2,1:T(8,128)(2,1)S(1)}, u32[]{:S(2)}, u32[]{:S(2)}) collective-permute-start(bf16[192,1,80]{0,2,1:T(8,128)(2,1)S(1)} %get-tuple-element.143), channel_id=1, source_target_pairs={{8,0},{16,8},{24,16},{9,1},{17,9},{25,17},{10,2},{18,10},{26,18},{... | collective-permute-start | bytes 92168 | tf_op jit(solution)/shard_map/ppermute | solution.py:21
  90.6 5.3 %collective-permute-start.10 = (bf16[96,4,16]{0,2,1:T(8,128)(2,1)S(1)}, bf16[96,4,16]{0,2,1:T(8,128)(2,1)S(1)}, u32[]{:S(2)}, u32[]{:S(2)}) collective-permute-start(bf16[96,4,16]{0,2,1:T(8,128)(2,1)S(1)} %get-tuple-element.49), channel_id=1, source_target_pairs={{0,1},{1,2},{2,3},{3,4},{4,5},{5,6},{6,7},{8,9},{9,10},{10,11},{11... | collective-permute-start | bytes 36872 | tf_op jit(solution)/shard_map/ppermute | solution.py:19
  92.8 5.4 %collective-permute-start.11 = (bf16[96,4,16]{0,2,1:T(8,128)(2,1)S(1)}, bf16[96,4,16]{0,2,1:T(8,128)(2,1)S(1)}, u32[]{:S(2)}, u32[]{:S(2)}) collective-permute-start(bf16[96,4,16]{0,2,1:T(8,128)(2,1)S(1)} %get-tuple-element.50), channel_id=1, source_target_pairs={{1,0},{2,1},{3,2},{4,3},{5,4},{6,5},{7,6},{9,8},{10,9},{11,10},{12... | collective-permute-start | bytes 36872 | tf_op jit(solution)/shard_map/ppermute | solution.py:21
  98.3 5.5 %collective-permute-start.12 = (bf16[96,1,288]{0,2,1:T(8,128)(2,1)S(1)}, bf16[96,1,288]{0,2,1:T(8,128)(2,1)S(1)}, u32[]{:S(2)}, u32[]{:S(2)}) collective-permute-start(bf16[96,1,288]{0,2,1:T(8,128)(2,1)S(1)} %get-tuple-element.47), channel_id=1, source_target_pairs={{0,8},{8,16},{16,24},{1,9},{9,17},{17,25},{2,10},{10,18},{18,26},{... | collective-permute-start | bytes 165896 | tf_op jit(solution)/shard_map/ppermute | solution.py:19
  101.7 5.7 %collective-permute-start.13 = (bf16[96,1,288]{0,2,1:T(8,128)(2,1)S(1)}, bf16[96,1,288]{0,2,1:T(8,128)(2,1)S(1)}, u32[]{:S(2)}, u32[]{:S(2)}) collective-permute-start(bf16[96,1,288]{0,2,1:T(8,128)(2,1)S(1)} %get-tuple-element.48), channel_id=1, source_target_pairs={{8,0},{16,8},{24,16},{9,1},{17,9},{25,17},{10,2},{18,10},{26,18},{... | collective-permute-start | bytes 165896 | tf_op jit(solution)/shard_map/ppermute | solution.py:21
  120.9 5.7 %collective-permute-start.14 = (bf16[32,4,16]{2,1,0:T(4,128)(2,1)S(1)}, bf16[32,4,16]{2,1,0:T(4,128)(2,1)S(1)}, u32[]{:S(2)}, u32[]{:S(2)}) collective-permute-start(bf16[32,4,16]{2,1,0:T(4,128)(2,1)S(1)} %get-tuple-element.202), channel_id=1, source_target_pairs={{0,1},{1,2},{2,3},{3,4},{4,5},{5,6},{6,7},{8,9},{9,10},{10,11},{11... | collective-permute-start | bytes 12296 | tf_op jit(solution)/shard_map/ppermute | solution.py:19
  124.1 5.6 %collective-permute-start.15 = (bf16[32,4,16]{2,1,0:T(4,128)(2,1)S(1)}, bf16[32,4,16]{2,1,0:T(4,128)(2,1)S(1)}, u32[]{:S(2)}, u32[]{:S(2)}) collective-permute-start(bf16[32,4,16]{2,1,0:T(4,128)(2,1)S(1)} %get-tuple-element.203), channel_id=1, source_target_pairs={{1,0},{2,1},{3,2},{4,3},{5,4},{6,5},{7,6},{9,8},{10,9},{11,10},{12... | collective-permute-start | bytes 12296 | tf_op jit(solution)/shard_map/ppermute | solution.py:21
  129.9 6.7 %collective-permute-start.16 = (bf16[32,1,288]{2,1,0:T(2,128)(2,1)S(1)}, bf16[32,1,288]{2,1,0:T(2,128)(2,1)S(1)}, u32[]{:S(2)}, u32[]{:S(2)}) collective-permute-start(bf16[32,1,288]{2,1,0:T(2,128)(2,1)S(1)} %get-tuple-element.140), channel_id=1, source_target_pairs={{0,8},{8,16},{16,24},{1,9},{9,17},{17,25},{2,10},{10,18},{18,26},{... | collective-permute-start | bytes 55304 | tf_op jit(solution)/shard_map/ppermute | solution.py:19
  133.2 5.4 %collective-permute-start.17 = (bf16[32,1,288]{2,1,0:T(2,128)(2,1)S(1)}, bf16[32,1,288]{2,1,0:T(2,128)(2,1)S(1)}, u32[]{:S(2)}, u32[]{:S(2)}) collective-permute-start(bf16[32,1,288]{2,1,0:T(2,128)(2,1)S(1)} %get-tuple-element.141), channel_id=1, source_target_pairs={{8,0},{16,8},{24,16},{9,1},{17,9},{25,17},{10,2},{18,10},{26,18},{... | collective-permute-start | bytes 55304 | tf_op jit(solution)/shard_map/ppermute | solution.py:21
  167.8 5.6 %collective-permute-start.18 = (bf16[64,2,8]{2,1,0:T(2,128)(2,1)S(1)}, bf16[64,2,8]{2,1,0:T(2,128)(2,1)S(1)}, u32[]{:S(2)}, u32[]{:S(2)}) collective-permute-start(bf16[64,2,8]{2,1,0:T(2,128)(2,1)S(1)} %get-tuple-element.270), channel_id=1, source_target_pairs={{0,1},{1,2},{2,3},{3,4},{4,5},{5,6},{6,7},{8,9},{9,10},{10,11},{11... | collective-permute-start | bytes 6152 | tf_op jit(solution)/shard_map/ppermute | solution.py:19
  170.0 5.6 %collective-permute-start.19 = (bf16[64,2,8]{2,1,0:T(2,128)(2,1)S(1)}, bf16[64,2,8]{2,1,0:T(2,128)(2,1)S(1)}, u32[]{:S(2)}, u32[]{:S(2)}) collective-permute-start(bf16[64,2,8]{2,1,0:T(2,128)(2,1)S(1)} %get-tuple-element.271), channel_id=1, source_target_pairs={{1,0},{2,1},{3,2},{4,3},{5,4},{6,5},{7,6},{9,8},{10,9},{11,10},{12... | collective-permute-start | bytes 6152 | tf_op jit(solution)/shard_map/ppermute | solution.py:21
  176.4 7.0 %collective-permute-start.20 = (bf16[64,1,80]{2,1,0:T(2,128)(2,1)}, bf16[64,1,80]{2,1,0:T(2,128)(2,1)}, u32[]{:S(2)}, u32[]{:S(2)}) collective-permute-start(bf16[64,1,80]{2,1,0:T(2,128)(2,1)} %get-tuple-element.268), channel_id=1, source_target_pairs={{0,8},{8,16},{16,24},{1,9},{9,17},{17,25},{2,10},{10,18},{18,26},{... | collective-permute-start | bytes 30728 | tf_op jit(solution)/shard_map/ppermute | solution.py:19
  179.7 5.6 %collective-permute-start.21 = (bf16[64,1,80]{2,1,0:T(2,128)(2,1)}, bf16[64,1,80]{2,1,0:T(2,128)(2,1)}, u32[]{:S(2)}, u32[]{:S(2)}) collective-permute-start(bf16[64,1,80]{2,1,0:T(2,128)(2,1)} %get-tuple-element.269), channel_id=1, source_target_pairs={{8,0},{16,8},{24,16},{9,1},{17,9},{25,17},{10,2},{18,10},{26,18},{... | collective-permute-start | bytes 30728 | tf_op jit(solution)/shard_map/ppermute | solution.py:21
  199.8 5.0 %all-to-all-start.1 = ((f32[4,1,512]{2,1,0:T(1,128)}), f32[4,1,512]{2,1,0:T(1,128)S(1)}, u32[]{:S(2)}, u32[]{:S(2)}) async-start(f32[4,1,512]{2,1,0:T(1,128)} %reshape.1248), calls=%async_computation.1 | async-start | bytes 16384 | tf_op jit(solution)/shard_map/all_to_all | solution.py:197
  203.1 36.9 %reduce-scatter.2.cloned.1.call-start = ((), (), s32[]{:S(2)}) async-start(), calls=%async_computation.3 | async-start | bytes 20480 | tf_op jit(solution)/shard_map/reduce_scatter | solution.py:207
  209.3 5.6 %collective-permute-start.22 = (bf16[32,4,4]{0,2,1:T(4,128)(2,1)S(1)}, bf16[32,4,4]{0,2,1:T(4,128)(2,1)S(1)}, u32[]{:S(2)}, u32[]{:S(2)}) collective-permute-start(bf16[32,4,4]{0,2,1:T(4,128)(2,1)S(1)} %get-tuple-element.305), channel_id=1, source_target_pairs={{0,1},{1,2},{2,3},{3,4},{4,5},{5,6},{6,7},{8,9},{9,10},{10,11},{11... | collective-permute-start | bytes 3080 | tf_op jit(solution)/shard_map/ppermute | solution.py:19
  211.2 5.3 %collective-permute-start.23 = (bf16[32,4,4]{0,2,1:T(4,128)(2,1)S(1)}, bf16[32,4,4]{0,2,1:T(4,128)(2,1)S(1)}, u32[]{:S(2)}, u32[]{:S(2)}) collective-permute-start(bf16[32,4,4]{0,2,1:T(4,128)(2,1)S(1)} %get-tuple-element.306), channel_id=1, source_target_pairs={{1,0},{2,1},{3,2},{4,3},{5,4},{6,5},{7,6},{9,8},{10,9},{11,10},{12... | collective-permute-start | bytes 3080 | tf_op jit(solution)/shard_map/ppermute | solution.py:21
  219.3 29.3 %copy-start.124 = (bf16[32,128]{1,0:T(8,128)(2,1)S(1)}, bf16[32,128]{1,0:T(8,128)(2,1)}, u32[]{:S(2)}) copy-start(bf16[32,128]{1,0:T(8,128)(2,1)} %copy-done.123) | copy-start | bytes 24580
  219.3 29.5 %copy-start.138 = (bf16[32,128]{1,0:T(8,128)(2,1)S(1)}, bf16[32,128]{1,0:T(8,128)(2,1)}, u32[]{:S(2)}) copy-start(bf16[32,128]{1,0:T(8,128)(2,1)} %copy-done.137) | copy-start | bytes 24580
  219.5 29.5 %copy-start.108 = (bf16[32,128]{1,0:T(8,128)(2,1)S(1)}, bf16[32,128]{1,0:T(8,128)(2,1)}, u32[]{:S(2)}) copy-start(bf16[32,128]{1,0:T(8,128)(2,1)} %copy-done.107) | copy-start | bytes 24580
  219.5 29.6 %copy-start.120 = (bf16[32,128]{1,0:T(8,128)(2,1)S(1)}, bf16[32,128]{1,0:T(8,128)(2,1)}, u32[]{:S(2)}) copy-start(bf16[32,128]{1,0:T(8,128)(2,1)} %copy-done.119) | copy-start | bytes 24580
  219.7 29.5 %copy-start.136 = (bf16[32,128]{1,0:T(8,128)(2,1)S(1)}, bf16[32,128]{1,0:T(8,128)(2,1)}, u32[]{:S(2)}) copy-start(bf16[32,128]{1,0:T(8,128)(2,1)} %copy-done.135) | copy-start | bytes 24580
  219.7 29.7 %copy-start.106 = (bf16[32,128]{1,0:T(8,128)(2,1)S(1)}, bf16[32,128]{1,0:T(8,128)(2,1)}, u32[]{:S(2)}) copy-start(bf16[32,128]{1,0:T(8,128)(2,1)} %copy-done.105) | copy-start | bytes 24580
  219.8 29.7 %copy-start.116 = (bf16[32,128]{1,0:T(8,128)(2,1)S(1)}, bf16[32,128]{1,0:T(8,128)(2,1)}, u32[]{:S(2)}) copy-start(bf16[32,128]{1,0:T(8,128)(2,1)} %copy-done.115) | copy-start | bytes 24580
  219.8 29.8 %copy-start.132 = (bf16[32,128]{1,0:T(8,128)(2,1)S(1)}, bf16[32,128]{1,0:T(8,128)(2,1)}, u32[]{:S(2)}) copy-start(bf16[32,128]{1,0:T(8,128)(2,1)} %copy-done.131) | copy-start | bytes 24580
  219.8 30.0 %copy-start.104 = (bf16[32,128]{1,0:T(8,128)(2,1)S(1)}, bf16[32,128]{1,0:T(8,128)(2,1)}, u32[]{:S(2)}) copy-start(bf16[32,128]{1,0:T(8,128)(2,1)} %copy-done.103) | copy-start | bytes 24580
  220.0 29.9 %copy-start.158 = (bf16[32,128]{1,0:T(8,128)(2,1)S(1)}, bf16[32,128]{1,0:T(8,128)(2,1)}, u32[]{:S(2)}) copy-start(bf16[32,128]{1,0:T(8,128)(2,1)} %copy-done.157) | copy-start | bytes 24580
  221.7 71.4 %all-reduce.14.cloned.1.call-start = ((), (), s32[]{:S(2)}) async-start(), calls=%async_computation.4 | async-start | bytes 229376 | tf_op jit(solution)/shard_map/psum | solution.py:210
  222.5 213.2 %all-reduce.16.cloned.1.call-start = ((), (), s32[]{:S(2)}) async-start(), calls=%async_computation.5 | async-start | bytes 4259840 | tf_op jit(solution)/shard_map/psum | solution.py:214
  241.2 8.9 %collective-permute-start.24 = (bf16[64,2,8]{2,1,0:T(2,128)(2,1)S(1)}, bf16[64,2,8]{2,1,0:T(2,128)(2,1)S(1)}, u32[]{:S(2)}, u32[]{:S(2)}) collective-permute-start(bf16[64,2,8]{2,1,0:T(2,128)(2,1)S(1)} %get-tuple-element.266), channel_id=1, source_target_pairs={{0,1},{1,2},{2,3},{3,4},{4,5},{5,6},{6,7},{8,9},{9,10},{10,11},{11... | collective-permute-start | bytes 6152 | tf_op jit(solution)/shard_map/ppermute | solution.py:19
  244.3 5.7 %collective-permute-start.25 = (bf16[64,2,8]{2,1,0:T(2,128)(2,1)S(1)}, bf16[64,2,8]{2,1,0:T(2,128)(2,1)S(1)}, u32[]{:S(2)}, u32[]{:S(2)}) collective-permute-start(bf16[64,2,8]{2,1,0:T(2,128)(2,1)S(1)} %get-tuple-element.267), channel_id=1, source_target_pairs={{1,0},{2,1},{3,2},{4,3},{5,4},{6,5},{7,6},{9,8},{10,9},{11,10},{12... | collective-permute-start | bytes 6152 | tf_op jit(solution)/shard_map/ppermute | solution.py:21
  250.3 7.3 %collective-permute-start.26 = (bf16[64,1,80]{2,1,0:T(2,128)(2,1)S(1)}, bf16[64,1,80]{2,1,0:T(2,128)(2,1)S(1)}, u32[]{:S(2)}, u32[]{:S(2)}) collective-permute-start(bf16[64,1,80]{2,1,0:T(2,128)(2,1)S(1)} %get-tuple-element.264), channel_id=1, source_target_pairs={{0,8},{8,16},{16,24},{1,9},{9,17},{17,25},{2,10},{10,18},{18,26},{... | collective-permute-start | bytes 30728 | tf_op jit(solution)/shard_map/ppermute | solution.py:19
  254.5 5.2 %collective-permute-start.27 = (bf16[64,1,80]{2,1,0:T(2,128)(2,1)S(1)}, bf16[64,1,80]{2,1,0:T(2,128)(2,1)S(1)}, u32[]{:S(2)}, u32[]{:S(2)}) collective-permute-start(bf16[64,1,80]{2,1,0:T(2,128)(2,1)S(1)} %get-tuple-element.265), channel_id=1, source_target_pairs={{8,0},{16,8},{24,16},{9,1},{17,9},{25,17},{10,2},{18,10},{26,18},{... | collective-permute-start | bytes 30728 | tf_op jit(solution)/shard_map/ppermute | solution.py:21
  (157 other events, 1779.3 us)
Sparse Core Ops, SparseCore 0:
  221.8 18.1 reduce-scatter.1
Sparse Core Ops, SparseCore 1:
  226.5 66.6 all-reduce.13
  299.5 136.0 all-reduce.15
where the time goes:
time: 452 us; the launch traced here: 448 us
  waiting for transfers between devices  214 us (47%)
  starting transfers between devices  84.2 us (19%)
  matrix products  77.2 us (17%)
  local copies, waits for them, and re-layouts  30.2 us (7%)
  other arithmetic  19.2 us (4%)
  between operations  19 us (4%)
  blocking collectives  4.92 us (1%)
    psum x1, waiting for transfers between devices, per_device(): grad_encoder = lax.psum(local_encoder, ('gx', 'gy'))  141 us
    ppermute x14, starting transfers between devices, extended_2(): lax.ppermute(tail, axis, [(i, (i + 1) % count) for i in range(ends)])  44.2 us
    ppermute x14, starting transfers between devices, extended_2(): lax.ppermute(head, axis, [((i + 1) % count, i) for i in range(ends)])  33.2 us
    ppermute x14, waiting for transfers between devices, extended_2(): lax.ppermute(head, axis, [((i + 1) % count, i) for i in range(ends)])  31.5 us
    dot_general x108, matrix products, weight_grad(): lax.dot_general(error_flat, tap_piece(shifted_set, a, b, c, row_count, co...  28.7 us
    dot_general x108, matrix products, conv_backward(): lax.dot_general(weight[:, tap_number * in_chan:(tap_number + 1) * in_chan...  26.3 us
    dot_general x108, matrix products, conv_forward(): jnp.dot(weight[:, tap_number * in_chan:(tap_number + 1) * in_chan], tap_p...  22.2 us
    psum x1, waiting for transfers between devices, per_device(): lax.psum((part_bottom * scale_low).astype(jnp.bfloat16), 'gy')  20.6 us
  transfers between devices with their start and end apart: 33, of which 17 were waited for; matrix products, arithmetic and copies ran while one was open for 6% of the time, Pallas kernels for 0%

commit v1 on v0

--- a/solution.py
+++ b/solution.py
@@ -171,7 +171,7 @@
         jnp.bfloat16
     )
     local_upper = weight_grad(ext_top, err_four, rows_fine, cols_fine, Z) * scale_fine
-    grad_upper = lax.psum(local_upper, ("gx", "gy"))
+    grad_upper = lax.psum(local_upper.astype(jnp.bfloat16), ("gx", "gy"))
     dcat_top = conv_backward(
         spatial_halo(err_four.reshape(top_chan, rows_fine, cols_fine * Z), Z),
         w_upper,
@@ -184,7 +184,10 @@
         block_sum(dcat_top[:mid_chan], Z).reshape(mid_chan, -1) * silu_slope(pre_three)
     ).astype(jnp.bfloat16)
     local_middle = weight_grad(ext_mid, err_three, rows_mid, cols_mid, depth_mid) * scale_mid
-    grad_middle = lax.psum(local_middle, ("gx", "gy"))
+    send_middle, grad_upper = lax.optimization_barrier(
+        (local_middle.astype(jnp.bfloat16), grad_upper)
+    )
+    grad_middle = lax.psum(send_middle, ("gx", "gy"))
     dcat_mid = conv_backward(
         spatial_halo(err_three.reshape(mid_chan, rows_mid, cols_mid * depth_mid), depth_mid),
         w_middle,
@@ -204,14 +207,26 @@
     partial_sum = conv_backward(err_ext, w_bottom, rows_all, cols_low, depth_low).reshape(
         -1, rows_all, cols_low * depth_low
     )
-    dpool_mid = lax.psum_scatter(
-        partial_sum.astype(jnp.bfloat16), "gx", scatter_dimension=1, tiled=True
+    dpool_parts = lax.all_to_all(
+        partial_sum.astype(jnp.bfloat16), "gx", split_axis=1, concat_axis=1, tiled=True
     ).astype(jnp.float32)
-    grad_bottom = lax.psum((part_bottom * scale_low).astype(jnp.bfloat16), "gy").astype(jnp.float32)
+    dpool_mid = dpool_parts.reshape(
+        dpool_parts.shape[0], lax.axis_size("gx"), rows_low, -1
+    ).sum(axis=1)
+    send_bottom, grad_middle = lax.optimization_barrier(
+        ((part_bottom * scale_low).astype(jnp.bfloat16), grad_middle)
+    )
+    grad_bottom = lax.psum(send_bottom, "gy")
     dact_one = dcat_mid[low_chan:] + upsample(dpool_mid, depth_low) / 8.0
     err_one = (dact_one.reshape(mid_chan, -1) * silu_slope(pre_one)).astype(jnp.bfloat16)
     local_encoder = weight_grad(ext_pool, err_one, rows_mid, cols_mid, depth_mid) * scale_mid
-    grad_encoder = lax.psum(local_encoder, ("gx", "gy"))
+    send_encoder, grad_bottom = lax.optimization_barrier(
+        (local_encoder.astype(jnp.bfloat16), grad_bottom)
+    )
+    grad_encoder = lax.psum(send_encoder, ("gx", "gy"))
+    grad_encoder, grad_bottom, grad_middle, grad_upper = (
+        grad.astype(jnp.float32) for grad in (grad_encoder, grad_bottom, grad_middle, grad_upper)
+    )
     dpool_top = conv_backward(
         spatial_halo(err_one.reshape(mid_chan, rows_mid, cols_mid * depth_mid), depth_mid),
         w_encoder,

time: 452 us -> 612 us (1.35)
  waiting for transfers between devices: 214 us -> 363 us
    psum x2 -> x4, waiting for transfers between devices: 161 us -> 323 us  [the longest x1 128 us: per_device(): grad_encoder = lax.psum(send_encoder, ('gx', 'gy'))]
    reduce_scatter x1 -> x0, waiting for transfers between devices: 17.5 us -> none  [per_device(): lax.psum_scatter(partial_sum.astype(jnp.bfloat16), 'gx', scatter_dimensio...]
  transfers between devices with their start and end apart: 33 -> 35, of which waited for: 17 -> 20; matrix products, arithmetic and copies ran while one was open for 6% -> 15% of each run, Pallas kernels for 0% -> 0%
where the time goes in v1:
time: 612 us; the launch traced here: 609 us
  waiting for transfers between devices  363 us (59%)
  starting transfers between devices  88 us (14%)
  matrix products  82.2 us (13%)
  local copies, waits for them, and re-layouts  34.3 us (6%)
  other arithmetic  19.7 us (3%)
  between operations  17.3 us (3%)
    psum x1, waiting for transfers between devices, per_device(): grad_encoder = lax.psum(send_encoder, ('gx', 'gy'))  128 us
    psum x1, waiting for transfers between devices, per_device(): grad_middle = lax.psum(send_middle, ('gx', 'gy'))  124 us
    psum x1, waiting for transfers between devices, per_device(): grad_bottom = lax.psum(send_bottom, 'gy')  70.9 us
    ppermute x14, starting transfers between devices, extended_2(): lax.ppermute(tail, axis, [(i, (i + 1) % count) for i in range(ends)])  41.8 us
    ppermute x14, starting transfers between devices, extended_2(): lax.ppermute(head, axis, [((i + 1) % count, i) for i in range(ends)])  34.1 us
    ppermute x14, waiting for transfers between devices, extended_2(): lax.ppermute(head, axis, [((i + 1) % count, i) for i in range(ends)])  33.6 us
    dot_general x108, matrix products, weight_grad(): lax.dot_general(error_flat, tap_piece(shifted_set, a, b, c, row_count, co...  32.7 us
    dot_general x108, matrix products, conv_backward(): lax.dot_general(weight[:, tap_number * in_chan:(tap_number + 1) * in_chan...  27.1 us
  transfers between devices with their start and end apart: 35, of which 20 were waited for; matrix products, arithmetic and copies ran while one was open for 15% of the time, Pallas kernels for 0%

profile of v1, /device:TPU:3, one launch (start us, length us, event | category | flops | bytes accessed | tf_op | source)
XLA Modules:
  0.0 608.9 jit_solution(14110399049150670056)
XLA Ops:
  8.6 3.2 collective-permute-start
  11.8 2.1 collective-permute-start.1
  17.2 5.1 collective-permute-start.2
  22.4 1.9 collective-permute-start.3
  24.9 2.5 collective-permute-done.3
  37.7 2.2 collective-permute-start.4
  39.9 3.1 collective-permute-start.5
  43.0 2.1 collective-permute-done.5
  45.2 4.9 all_gather.3
  56.5 3.4 all-to-all-start
  60.1 2.9 all-to-all-done
  63.3 3.2 collective-permute-start.6
  66.4 2.1 collective-permute-start.7
  68.6 3.1 collective-permute-done.7
  71.9 3.7 collective-permute-start.8
  75.5 1.9 collective-permute-start.9
  77.6 3.3 collective-permute-done.9
  89.7 2.2 collective-permute-start.10
  92.0 3.1 collective-permute-start.11
  95.1 2.3 collective-permute-done.11
  97.5 3.3 collective-permute-start.12
  100.8 2.1 collective-permute-start.13
  103.0 3.5 collective-permute-done.13
  123.1 3.2 collective-permute-start.14
  126.3 2.1 collective-permute-start.15
  129.5 2.3 collective-permute-done.15
  132.0 3.3 collective-permute-start.16
  135.3 1.9 collective-permute-start.17
  138.7 2.1 collective-permute-done.17
  172.5 2.2 collective-permute-start.18
  174.7 3.3 collective-permute-start.19
  178.1 2.5 collective-permute-done.19
  181.5 3.0 collective-permute-start.20
  184.4 2.0 collective-permute-start.21
  211.1 3.2 all-to-all-start.1
  220.5 2.0 collective-permute-start.22
  222.5 3.3 collective-permute-start.23
  233.0 5.4 all-to-all-start.2
  239.1 2.6 all-to-all-done.2
  245.7 1.9 collective-permute-start.24
  247.6 3.4 collective-permute-start.25
  251.1 2.1 collective-permute-done.25
  253.4 3.3 collective-permute-start.26
  256.7 1.9 collective-permute-start.27
  259.3 2.6 collective-permute-done.27
  273.5 124.3 %all-reduce.17.cloned.1.call-done = bf16[64,5184]{1,0:T(8,128)(2,1)} async-done(((bf16[64,5184]{1,0:T(8,128)(2,1)}), bf16[64,5184]{1,0:T(8,128)(2,1)}) %all-reduce.17.cloned.1.call-update) | async-done | bytes 663568 | tf_op jit(solution)/shard_map/psum | solution.py:190
  398.2 70.9 %all-reduce.19.cloned.1.call-done = bf16[32,1728]{1,0:T(8,128)(2,1)} async-done(((bf16[32,1728]{1,0:T(8,128)(2,1)}), bf16[32,1728]{1,0:T(8,128)(2,1)}) %all-reduce.19.cloned.1.call-update) | async-done | bytes 110608 | tf_op jit(solution)/shard_map/psum | solution.py:219
  472.8 127.9 %all-reduce.21.cloned.1.call-done = bf16[64,864]{0,1:T(8,128)(2,1)} async-done(((bf16[64,864]{0,1:T(8,128)(2,1)}), bf16[64,864]{0,1:T(8,128)(2,1)}) %all-reduce.21.cloned.1.call-update) | async-done | bytes 110608 | tf_op jit(solution)/shard_map/psum | solution.py:226
  (972 shorter events, 141.9 us)
Async XLA Ops:
  8.6 6.5 %collective-permute-start = (bf16[32,2,8]{0,2,1:T(8,128)(2,1)S(1)}, bf16[32,2,8]{0,2,1:T(8,128)(2,1)S(1)}, u32[]{:S(2)}, u32[]{:S(2)}) collective-permute-start(bf16[32,2,8]{0,2,1:T(8,128)(2,1)S(1)} %get-tuple-element.310), channel_id=1, source_target_pairs={{0,1},{1,2},{2,3},{3,4},{4,5},{5,6},{6,7},{8,9},{9,10},{10,11},{11... | collective-permute-start | bytes 3080 | tf_op jit(solution)/shard_map/ppermute | solution.py:19
  11.8 5.3 collective-permute-start.1
  14.5 35.7 %copy-start.164 = (pred[24]{0:T(512)(128)(4,1)}, pred[24]{0:T(512)(128)(4,1)S(1)}, u32[]{:S(2)}) copy-start(pred[24]{0:T(512)(128)(4,1)S(1)} %get-tuple-element.335) | copy-start | bytes 76
  14.5 35.7 %copy-start.166 = (pred[24]{0:T(512)(128)(4,1)}, pred[24]{0:T(512)(128)(4,1)S(1)}, u32[]{:S(2)}) copy-start(pred[24]{0:T(512)(128)(4,1)S(1)} %get-tuple-element.336) | copy-start | bytes 76
  17.2 7.6 %collective-permute-start.2 = (bf16[32,1,80]{2,0,1:T(8,128)(2,1)S(1)}, bf16[32,1,80]{2,0,1:T(8,128)(2,1)S(1)}, u32[]{:S(2)}, u32[]{:S(2)}) collective-permute-start(bf16[32,1,80]{2,0,1:T(8,128)(2,1)S(1)} %get-tuple-element.316), channel_id=1, source_target_pairs={{0,8},{8,16},{16,24},{1,9},{9,17},{17,25},{2,10},{10,18},{18,26},{... | collective-permute-start | bytes 15368 | tf_op jit(solution)/shard_map/ppermute | solution.py:19
  22.4 5.0 collective-permute-start.3
  37.7 5.3 collective-permute-start.4
  39.9 5.2 collective-permute-start.5
  50.5 27.0 %copy-start.48 = (bf16[64,4,16]{0,2,1:T(8,128)(2,1)}, bf16[64,4,16]{0,2,1:T(8,128)(2,1)S(1)}, u32[]{:S(2)}) copy-start(bf16[64,4,16]{0,2,1:T(8,128)(2,1)S(1)} %get-tuple-element.254) | copy-start | bytes 24580
  50.5 27.0 %copy-start.50 = (bf16[64,4,16]{0,2,1:T(8,128)(2,1)}, bf16[64,4,16]{0,2,1:T(8,128)(2,1)S(1)}, u32[]{:S(2)}) copy-start(bf16[64,4,16]{0,2,1:T(8,128)(2,1)S(1)} %get-tuple-element.255) | copy-start | bytes 24580
  50.5 27.0 %copy-start.52 = (bf16[64,4,16]{0,2,1:T(8,128)(2,1)}, bf16[64,4,16]{0,2,1:T(8,128)(2,1)S(1)}, u32[]{:S(2)}) copy-start(bf16[64,4,16]{0,2,1:T(8,128)(2,1)S(1)} %get-tuple-element.256) | copy-start | bytes 24580
  50.5 27.0 %copy-start.54 = (bf16[64,4,16]{0,2,1:T(8,128)(2,1)}, bf16[64,4,16]{0,2,1:T(8,128)(2,1)S(1)}, u32[]{:S(2)}) copy-start(bf16[64,4,16]{0,2,1:T(8,128)(2,1)S(1)} %get-tuple-element.257) | copy-start | bytes 24580
  50.6 27.0 %copy-start.84 = (bf16[64,4,16]{0,2,1:T(8,128)(2,1)}, bf16[64,4,16]{0,2,1:T(8,128)(2,1)S(1)}, u32[]{:S(2)}) copy-start(bf16[64,4,16]{0,2,1:T(8,128)(2,1)S(1)} %get-tuple-element.247) | copy-start | bytes 24580
  50.6 27.0 %copy-start.86 = (bf16[64,4,16]{0,2,1:T(8,128)(2,1)}, bf16[64,4,16]{0,2,1:T(8,128)(2,1)S(1)}, u32[]{:S(2)}) copy-start(bf16[64,4,16]{0,2,1:T(8,128)(2,1)S(1)} %get-tuple-element.248) | copy-start | bytes 24580
  50.6 27.0 %copy-start.88 = (bf16[64,4,16]{0,2,1:T(8,128)(2,1)}, bf16[64,4,16]{0,2,1:T(8,128)(2,1)S(1)}, u32[]{:S(2)}) copy-start(bf16[64,4,16]{0,2,1:T(8,128)(2,1)S(1)} %get-tuple-element.249) | copy-start | bytes 24580
  50.6 27.0 %copy-start.90 = (bf16[64,4,16]{0,2,1:T(8,128)(2,1)}, bf16[64,4,16]{0,2,1:T(8,128)(2,1)S(1)}, u32[]{:S(2)}) copy-start(bf16[64,4,16]{0,2,1:T(8,128)(2,1)S(1)} %get-tuple-element.250) | copy-start | bytes 24580
  50.6 27.0 %copy-start.92 = (bf16[64,4,16]{0,2,1:T(8,128)(2,1)}, bf16[64,4,16]{0,2,1:T(8,128)(2,1)S(1)}, u32[]{:S(2)}) copy-start(bf16[64,4,16]{0,2,1:T(8,128)(2,1)S(1)} %get-tuple-element.251) | copy-start | bytes 24580
  50.6 27.0 %copy-start.94 = (bf16[64,4,16]{0,2,1:T(8,128)(2,1)}, bf16[64,4,16]{0,2,1:T(8,128)(2,1)S(1)}, u32[]{:S(2)}) copy-start(bf16[64,4,16]{0,2,1:T(8,128)(2,1)S(1)} %get-tuple-element.252) | copy-start | bytes 24580
  56.5 6.5 %all-to-all-start = ((bf16[4,2,256]{2,1,0:T(2,128)(2,1)}), bf16[4,2,256]{2,1,0:T(2,128)(2,1)S(1)}, u32[]{:S(2)}, u32[]{:S(2)}) async-start(bf16[4,2,256]{2,1,0:T(2,128)(2,1)} %reshape.1249), calls=%async_computation | async-start | bytes 8192 | tf_op jit(solution)/shard_map/all_to_all | solution.py:157
  59.9 212.9 %all-reduce.15.cloned.1.call-start = ((), (), s32[]{:S(2)}) async-start(), calls=%async_computation.3 | async-start | bytes 344064 | tf_op jit(solution)/shard_map/psum | solution.py:174
  63.3 5.3 collective-permute-start.6
  66.4 5.3 collective-permute-start.7
  71.9 5.6 collective-permute-start.8
  75.5 5.3 collective-permute-start.9
  89.7 5.3 collective-permute-start.10
  92.0 5.4 collective-permute-start.11
  97.5 5.5 collective-permute-start.12
  100.8 5.7 collective-permute-start.13
  123.1 6.5 %collective-permute-start.14 = (bf16[32,4,16]{2,1,0:T(4,128)(2,1)S(1)}, bf16[32,4,16]{2,1,0:T(4,128)(2,1)S(1)}, u32[]{:S(2)}, u32[]{:S(2)}) collective-permute-start(bf16[32,4,16]{2,1,0:T(4,128)(2,1)S(1)} %get-tuple-element.211), channel_id=1, source_target_pairs={{0,1},{1,2},{2,3},{3,4},{4,5},{5,6},{6,7},{8,9},{9,10},{10,11},{11... | collective-permute-start | bytes 12296 | tf_op jit(solution)/shard_map/ppermute | solution.py:19
  126.3 5.6 collective-permute-start.15
  132.0 6.6 %collective-permute-start.16 = (bf16[32,1,288]{2,1,0:T(2,128)(2,1)S(1)}, bf16[32,1,288]{2,1,0:T(2,128)(2,1)S(1)}, u32[]{:S(2)}, u32[]{:S(2)}) collective-permute-start(bf16[32,1,288]{2,1,0:T(2,128)(2,1)S(1)} %get-tuple-element.149), channel_id=1, source_target_pairs={{0,8},{8,16},{16,24},{1,9},{9,17},{17,25},{2,10},{10,18},{18,26},{... | collective-permute-start | bytes 55304 | tf_op jit(solution)/shard_map/ppermute | solution.py:19
  135.3 5.4 collective-permute-start.17
  172.5 5.6 collective-permute-start.18
  174.7 5.9 collective-permute-start.19
  181.5 6.7 %collective-permute-start.20 = (bf16[64,1,80]{2,1,0:T(2,128)(2,1)}, bf16[64,1,80]{2,1,0:T(2,128)(2,1)}, u32[]{:S(2)}, u32[]{:S(2)}) collective-permute-start(bf16[64,1,80]{2,1,0:T(2,128)(2,1)} %get-tuple-element.277), channel_id=1, source_target_pairs={{0,8},{8,16},{16,24},{1,9},{9,17},{17,25},{2,10},{10,18},{18,26},{... | collective-permute-start | bytes 30728 | tf_op jit(solution)/shard_map/ppermute | solution.py:19
  184.4 5.6 collective-permute-start.21
  211.1 4.9 all-to-all-start.1
  220.5 5.6 collective-permute-start.22
  222.5 5.3 collective-permute-start.23
  233.0 8.6 %all-to-all-start.2 = ((bf16[4,2,512]{2,1,0:T(2,128)(2,1)}), bf16[4,2,512]{2,1,0:T(2,128)(2,1)S(1)}, u32[]{:S(2)}, u32[]{:S(2)}) async-start(bf16[4,2,512]{2,1,0:T(2,128)(2,1)} %reshape.1253), calls=%async_computation.2 | async-start | bytes 16384 | tf_op jit(solution)/shard_map/all_to_all | solution.py:210
  238.4 159.4 %all-reduce.17.cloned.1.call-start = ((), (), s32[]{:S(2)}) async-start(), calls=%async_computation.4 | async-start | bytes 1343488 | tf_op jit(solution)/shard_map/psum | solution.py:190
  245.7 5.4 collective-permute-start.24
  247.6 5.6 collective-permute-start.25
  253.4 5.9 collective-permute-start.26
  256.7 5.2 collective-permute-start.27
  272.8 196.3 %all-reduce.19.cloned.1.call-start = ((), (), s32[]{:S(2)}) async-start(), calls=%async_computation.5 | async-start | bytes 229376 | tf_op jit(solution)/shard_map/psum | solution.py:219
  273.5 196.7 %copy-start.45 = (bf16[32,2592]{1,0:T(8,128)(2,1)S(1)}, bf16[32,2592]{1,0:T(8,128)(2,1)}, u32[]{:S(2)}) copy-start(bf16[32,2592]{1,0:T(8,128)(2,1)} %all-reduce.15.cloned.1.call-done) | copy-start | bytes 497668
  397.8 202.8 %all-reduce.21.cloned.1.call-start = ((), (), s32[]{:S(2)}) async-start(), calls=%async_computation.6 | async-start | bytes 442368 | tf_op jit(solution)/shard_map/psum | solution.py:226
  (163 other events, 1525.7 us)
Sparse Core Ops, SparseCore 0:
  138.1 121.9 all-reduce.14
  272.9 124.8 all-reduce.16
  402.1 66.9 all-reduce.18
  475.1 125.5 all-reduce.20
